TPU v7x, 256 devices: a whole 4x4x8 slice. The times are simulated.
256 devices in a mesh: seq: 32 (over x, z), head: 8 (over y, core).
Axes of the slice: x: 4, y: 4, z: 8, core: 2. Of those that a mesh axis runs over, the one named last changes fastest.
Arguments:
- inputs: bfloat16 [16384, 2048], P('seq'), may hold values from -11 to 11
- out_grad: bfloat16 [16384, 2048], P('seq'), may hold values from -6 to 6
- w_query: bfloat16 [2048, 1024], P(None, 'head'), may hold values from -1 to 1
- w_key: bfloat16 [2048, 512], P(None, 'head'), may hold values from -1 to 1
- w_value: bfloat16 [2048, 512], P(None, 'head'), may hold values from -0.125 to 0.125
- w_output: bfloat16 [1024, 2048], P('head'), may hold values from -0.1875 to 0.1875
Outputs:
- grad_inputs: bfloat16 [16384, 2048], P('seq', 'head')
- grad_query: float32 [2048, 1024], P('seq', 'head')
- grad_key: float32 [2048, 512], P('seq', 'head')
- grad_value: float32 [2048, 512], P('seq', 'head')
- grad_output: float32 [1024, 2048], P('head', 'seq')
All inputs are finite; a program needn't handle non-finite values.
Results may differ from a plain program's by a relative error of at most 0.04.
Values may be sent and summed in bfloat16 or wider, within the bound.
A program may use at most 64 MiB of HBM per device.

v0:
```python
import functools

import jax
import jax.numpy as jnp
from jax import lax
from jax.experimental import pallas as pl
from jax.experimental.pallas import tpu as pltpu
from jax.sharding import PartitionSpec as P

HD = 64
NX, NZ, NH = 4, 8, 8
ROPE_BASE = 500000.0
NEG = -1e30
F32, BF16 = jnp.float32, jnp.bfloat16
MESH = pl.DeviceIdType.MESH


def rotary(positions):
    half_dim = HD // 2
    frequency = ROPE_BASE ** (-(jnp.arange(half_dim, dtype=jnp.float32) * 2.0 / HD))
    angles = positions[:, None] * frequency[None, :]
    return jnp.cos(angles), jnp.sin(angles)


def mod(value, size):
    return lax.rem(value + 2 * size, size)


class Links:
    def __init__(self, send_sems, recv_sems):
        self.send_sems, self.recv_sems = send_sems, recv_sems
        self.used, self.open = 0, []

    def send(self, src, dst, device):
        index = self.used
        self.used += 1
        copy = pltpu.make_async_remote_copy(
            src_ref=src,
            dst_ref=dst,
            send_sem=self.send_sems.at[index],
            recv_sem=self.recv_sems.at[index],
            device_id=device,
            device_id_type=MESH,
        )
        copy.start()
        self.open.append(copy)
        return index

    def arrived(self, index, landing):
        pltpu.make_async_copy(landing, landing, self.recv_sems.at[index]).wait()

    def drain(self):
        for copy in self.open:
            copy.wait_send()
        self.open = []


def together(*streams):
    streams = list(streams)
    while streams:
        for stream in list(streams):
            try:
                next(stream)
            except StopIteration:
                streams.remove(stream)


def gather_ring(links, slots, own, where, size, right, left, cut):
    far = size // 2
    low, high = cut
    held_r, held_l = own, own
    for step in range(1, far + 1):
        slot_r, slot_l = mod(where - step + 1, size), mod(where + step - 1, size)
        if step == far:
            held_r, held_l = low(held_r), high(held_l)
            place_r, place_l = low(slots(slot_r)), high(slots(slot_l))
        else:
            place_r, place_l = slots(slot_r), slots(slot_l)
        got_r = links.send(held_r, place_r, right)
        got_l = links.send(held_l, place_l, left)
        yield
        held_r, held_l = slots(mod(where - step, size)), slots(mod(where + step, size))
        if step == far:
            links.arrived(got_r, low(held_r))
            links.arrived(got_l, high(held_l))
        else:
            links.arrived(got_r, held_r)
            links.arrived(got_l, held_l)


def scatter_ring(links, mine, snd, from_left, from_right, where, size, right, left, cut, finish):
    far = size // 2
    low, high = cut
    owner = mod(where + far, size)
    snd(owner)[...] = mine(owner)[...].astype(BF16)
    got_r = links.send(low(snd(owner)), low(from_left(0)), right)
    got_l = links.send(high(snd(owner)), high(from_right(0)), left)
    for step in range(2, far + 1):
        yield
        for got, came, place, sign, part, target in (
            (got_r, from_left, from_left, 1, low, right),
            (got_l, from_right, from_right, -1, high, left),
        ):
            owner = mod(where + sign * (far - step + 1), size)
            if step == 2:
                links.arrived(got, part(came(0)))
                other = high if part is low else low
                part(snd(owner))[...] = (
                    part(mine(owner))[...].astype(F32) + part(came(0))[...].astype(F32)
                ).astype(BF16)
                other(snd(owner))[...] = other(mine(owner))[...].astype(BF16)
            else:
                links.arrived(got, came(step - 2))
                snd(owner)[...] = (
                    mine(owner)[...].astype(F32) + came(step - 2)[...].astype(F32)
                ).astype(BF16)
            sent = links.send(snd(owner), place(step - 1), target)
            if sign == 1:
                got_r = sent
            else:
                got_l = sent
    yield
    links.arrived(got_r, from_left(far - 1))
    links.arrived(got_l, from_right(far - 1))
    finish(
        mine(where)[...].astype(F32)
        + from_left(far - 1)[...].astype(F32)
        + from_right(far - 1)[...].astype(F32)
    )


def seq_place():
    me = lax.axis_index("seq")
    return lax.div(me, NZ), lax.rem(me, NZ)


def seq_dev(x, z):
    return {"seq": x * NZ + z}


def nn(a, b):
    return lax.dot_general(a, b, (((1,), (0,)), ((), ())), preferred_element_type=F32)


def nt(a, b):
    return lax.dot_general(a, b, (((1,), (1,)), ((), ())), preferred_element_type=F32)


def fold(values, op):
    return op(values.reshape(values.shape[0] // 8, 8, values.shape[1]), axis=0)


def layer_kernel(
    inputs, out_grad, w_query, w_key, w_value, w_output, cos_t, sin_t,
    gi_out, gq_out, gk_out, gv_out, go_out,
    x_v, g_v, w_cat, wk_v, wv_v, wo_v, w_all, x_t,
    q_own, do_own, kv_own,
    qg, dg, kv, kvt, both, probs, tops, stats, lse, delta, o_sum, dq_sum, dkv,
    ring_o, o_in, ring_q, q_in, o_t, g_t,
    dkv_snd, dkv_l, dkv_r, dkv_back, dkv_land,
    proj_o, po_snd, po_l, po_r, po_x, po_xs, po_xi,
    proj_kv, pk_snd, pk_l, pk_r, pk_x, pk_xs, pk_xi,
    proj_q, pq_snd, pq_l, pq_r, pq_z, pq_zi,
    g_all, gi_sum,
    send_sems, recv_sems, copy_sems,
):
    x, z = seq_place()
    head = lax.axis_index("head")
    y, core = lax.div(head, 2), lax.rem(head, 2)
    chunk, lanes = kv_own.shape[1], q_own.shape[2]
    far_x, far_z = NX - 1 - x, NZ - 1 - z
    right_x, left_x = seq_dev(mod(x + 1, NX), z), seq_dev(mod(x - 1, NX), z)
    across_x, mirror_x = seq_dev(mod(x + 2, NX), z), seq_dev(far_x, z)
    right_z, left_z = seq_dev(x, mod(z + 1, NZ)), seq_dev(x, mod(z - 1, NZ))
    mirror_z = seq_dev(x, far_z)
    others = [{"head": mod(head + step, NH)} for step in range(1, NH)]
    right_y, left_y = {"head": mod(y + 1, 4) * 2 + core}, {"head": mod(y - 1, 4) * 2 + core}
    twin = {"head": y * 2 + 1 - core}

    loads = [
        pltpu.make_async_copy(source, target, copy_sems.at[n])
        for n, (source, target) in enumerate(
            (
                (w_query, w_cat.at[:, 0:128]),
                (w_key, wk_v),
                (w_value, wv_v),
                (inputs, x_v),
                (w_output, wo_v),
                (out_grad, g_v),
            )
        )
    ]
    for load in loads:
        load.start()
    partners = (
        [seq_dev(mod(x + step, NX), z) for step in range(1, NX)]
        + [seq_dev(x, mod(z + step, NZ)) for step in range(1, NZ)]
        + [seq_dev(mod(x + step, NX), far_z) for step in range(1, NX)]
        + others
    )
    barrier = pltpu.get_barrier_semaphore()
    for device in partners:
        pl.semaphore_signal(barrier, inc=1, device_id=device, device_id_type=MESH)
    links = Links(send_sems, recv_sems)

    for load in loads[:3]:
        load.wait()
    w_kv = jnp.concatenate([wk_v[...], wv_v[...]], 0)
    w_cat[:, 128:256] = w_kv.astype(F32).T.astype(BF16)
    loads[3].wait()

    def turn(rows, a, sign):
        cos, sin = (table[:, a * chunk : (a + 1) * chunk] for table in (cos_t, sin_t))
        front, back = rows[0:32], rows[32:64]
        return jnp.concatenate([front * cos - sign * back * sin, back * cos + sign * front * sin], 0)

    for a in range(2):
        rows = nn(x_v[a * chunk : (a + 1) * chunk, :], w_cat[...]).T
        q = jnp.concatenate([turn(rows[0:64], a, 1.0), turn(rows[64:128], a, 1.0)], 1).astype(BF16)
        q_own[a] = q * jnp.asarray(0.125, BF16)
        kv_own[a] = jnp.concatenate([turn(rows[128:192], a, 1.0), rows[192:256]], 0).T.astype(BF16)
    qg[x, 0] = q_own[0]
    kv[z, 0] = kv_own[0]
    pl.semaphore_wait(barrier, len(partners))

    sent_q = links.send(q_own.at[1], qg.at[x, 1], mirror_z)
    sent_kv = links.send(kv_own.at[1], kv.at[z, 1], mirror_x)
    rows_q = (lambda ref: ref.at[0:32], lambda ref: ref.at[32:64])
    rows_k = (lambda ref: ref.at[0 : chunk // 2], lambda ref: ref.at[chunk // 2 : chunk])

    def ring_x(ref, a, own):
        return gather_ring(links, lambda i: ref.at[i, a], own, x, NX, right_x, left_x, rows_q)

    def ring_z(a, own):
        return gather_ring(links, lambda i: kv.at[i, a], own, z, NZ, right_z, left_z, rows_k)

    def pump(*rings):
        for ring in rings:
            next(ring, None)

    q_a, k_a = ring_x(qg, 0, q_own.at[0]), ring_z(0, kv_own.at[0])
    q_b, k_b = ring_x(qg, 1, qg.at[x, 1]), ring_z(1, kv.at[z, 1])
    d_a, d_b = ring_x(dg, 0, do_own.at[0]), ring_x(dg, 1, dg.at[x, 1])
    pump(q_a, k_a)
    for load in loads[4:]:
        load.wait()
    for a in range(2):
        rows = nt(wo_v[...], g_v[a * chunk : (a + 1) * chunk, :]).astype(BF16)
        do_own[a] = jnp.concatenate([rows[0:64], rows[64:128]], 1)
    dg[x, 0] = do_own[0]
    links.arrived(sent_q, qg.at[x, 1])
    pump(q_b)
    links.arrived(sent_kv, kv.at[z, 1])
    pump(k_b)
    sent_do = links.send(do_own.at[1], dg.at[x, 1], mirror_z)
    dkv[...] = jnp.zeros(dkv.shape, F32)
    o_sum[...] = jnp.zeros(o_sum.shape, F32)
    dq_sum[...] = jnp.zeros(dq_sum.shape, F32)
    both[...] = jnp.zeros(both.shape, BF16)
    stats[x, 0] = jnp.full(stats.shape[2:], NEG, F32)
    stats[x, 1] = jnp.zeros(stats.shape[2:], F32)
    pump(q_a, k_a, q_b, k_b, d_a)
    links.arrived(sent_do, dg.at[x, 1])
    pump(d_b)

    def flip(n, _):
        part = pl.ds(pl.multiple_of(n * 128, 128), 128)
        x_t[part, :] = x_v[:, part].astype(F32).T.astype(BF16)
        return 0

    lax.fori_loop(0, x_t.shape[0] // 128, flip, 0)
    pump(q_a, q_b)

    def full_tiles(zc):
        tiles = []
        for n in range(3):
            first = n < far_x
            half, block = jnp.where(first, 0, 1), jnp.where(first, x + 1 + n, n + 1)
            tiles += [(half, block, a, zc * 6 + n * 2 + a) for a in range(2)]
        return tiles

    def cross_tiles(zc, a):
        base = 6 * NZ + (0 if a == 0 else 2 * z + 1) + 2 * zc
        return [(0, x, a, base), (1, far_x, a, base + 1)]

    def forward(zc, tiles, cut=()):
        found = []
        for n, (half, block, a, place) in enumerate(tiles):
            s = nn(kv[zc, half][:, 0:64], qg[block, a])
            if n in cut:
                key = lax.broadcasted_iota(jnp.int32, (chunk, lanes), 0)
                row = lax.rem(lax.broadcasted_iota(jnp.int32, (chunk, lanes), 1), chunk)
                on_diagonal = zc == (z if a == 0 else far_z)
                s = jnp.where(row - key >= jnp.where(on_diagonal, 0, -chunk), s, NEG)
            found.append(s)
        highs = [jnp.max(fold(s, jnp.max), axis=0, keepdims=True) for s in found]
        raised = [jnp.exp(s - high) for s, high in zip(found, highs)]
        lows = [p.astype(BF16) for p in raised]
        totals = [jnp.sum(fold(p, jnp.sum), axis=0, keepdims=True) for p in raised]
        for (_, _, _, place), low, high in zip(tiles, lows, highs):
            probs[place] = low
            tops[pl.ds(place, 1), :] = high
        outs = [nn(kvt[zc, half, 64:128, :], low) for (half, _, _, _), low in zip(tiles, lows)]
        for (_, block, a, _), high, total, out in zip(tiles, highs, totals, outs):
            group = pl.ds(block * 2 + a, 1)
            old = stats[x, 0, group, :]
            top = jnp.maximum(old, high)
            keep, add = jnp.exp(old - top), jnp.exp(high - top)
            stats[x, 0, group, :] = top
            stats[x, 1, group, :] = stats[x, 1, group, :] * keep + total * add
            o_sum[block, a] = o_sum[block, a] * keep + out * add

    def forward_slot(zc):
        for half in range(2):
            kvt[zc, half] = kv[zc, half].astype(F32).T.astype(BF16)
        forward(zc, full_tiles(zc))
        pl.when(zc < z)(lambda: forward(zc, cross_tiles(zc, 0)))
        pl.when(zc == z)(lambda: forward(zc, cross_tiles(zc, 0)[:1], (0,)))
        pl.when(zc <= far_z)(lambda: forward(zc, cross_tiles(zc, 1), (1,)))

    def slots(work, distances):
        def one(n, _):
            work(mod(z + distances[0] + n * (distances[-1] - distances[0]), NZ))
            return 0

        lax.fori_loop(0, len(distances), one, 0)

    slots(forward_slot, (0,))
    pump(k_a, k_b, d_a, d_b)
    slots(forward_slot, (1, -1))
    pump(k_a, k_b, d_a, d_b)
    slots(forward_slot, (2, -2))
    pump(k_a, k_b)
    slots(forward_slot, (3, -3))
    slots(forward_slot, (4,))

    weights = []
    for step in range(1, NH):
        rows = pl.ds(pl.multiple_of(mod(head + step, NH) * w_all.shape[1], w_all.shape[1]), w_all.shape[1])
        weights.append((links.send(w_cat.at[rows], w_all.at[head], others[step - 1]), step))
    rows = pl.ds(pl.multiple_of(head * w_all.shape[1], w_all.shape[1]), w_all.shape[1])
    w_all[head] = w_cat[rows, :]

    for block in range(NX):
        for a in range(2):
            group = block * 2 + a
            stats[x, 2, group : group + 1, :] = jnp.sum(
                o_sum[block, a] * dg[block, a].astype(F32), axis=0, keepdims=True
            )
    shares = [
        (links.send(stats.at[x], stats.at[x], device), mod(x - step, NX))
        for step, device in ((1, right_x), (2, across_x), (3, left_x))
    ]
    for block in range(NX):
        for a in range(2):
            both[block, 0:64, a * lanes : (a + 1) * lanes] = qg[block, a]
            both[block, 64:128, (2 + a) * lanes : (3 + a) * lanes] = dg[block, a]
    for index, source in shares:
        links.arrived(index, stats.at[source])
    top = functools.reduce(jnp.maximum, [stats[n, 0] for n in range(NX)])
    part = [jnp.exp(stats[n, 0] - top) for n in range(NX)]
    total = sum(stats[n, 1] * part[n] for n in range(NX))
    lse[...] = top + jnp.log(total)
    delta[...] = sum(stats[n, 2] * part[n] for n in range(NX)) / total
    share = jnp.exp(stats[x, 0] - lse[...])
    for block in range(NX):
        for a in range(2):
            group = block * 2 + a
            ring_o[block, a] = (o_sum[block, a] * share[group : group + 1]).astype(BF16)

    def backward_tile(zc, half, block, a, place):
        group = pl.ds(block * 2 + a, 1)
        scale = jnp.exp(tops[pl.ds(place, 1), :] - lse[group, :])
        p = probs[place] * scale.astype(BF16)
        dp = nn(kv[zc, half], both[block, :, (2 + a) * lanes : (3 + a) * lanes])
        return p, p * (dp - delta[group, :]).astype(BF16)

    def backward_full(zc):
        tiles = full_tiles(zc)
        done = [backward_tile(zc, *tile) for tile in tiles]
        for (half, block, a, _), (_, ds) in zip(tiles, done):
            dq_sum[block, a] += nn(kvt[zc, half, 0:64, :], ds)
        for n in range(3):
            half, block = tiles[2 * n][:2]
            (p0, ds0), (p1, ds1) = done[2 * n], done[2 * n + 1]
            dkv[zc, half] += nt(jnp.concatenate([ds0, ds1, p0, p1], 1), both[block])

    def backward_some(zc, tiles):
        done = [backward_tile(zc, *tile) for tile in tiles]
        for (half, block, a, _), (p, ds) in zip(tiles, done):
            dq_sum[block, a] += nn(kvt[zc, half, 0:64, :], ds)
            dkv[zc, half] += nt(ds, both[block, :, a * lanes : (a + 1) * lanes]) + nt(
                p, both[block, :, (2 + a) * lanes : (3 + a) * lanes]
            )

    def backward_slot(zc):
        backward_full(zc)
        pl.when(zc < z)(lambda: backward_some(zc, cross_tiles(zc, 0)))
        pl.when(zc == z)(lambda: backward_some(zc, cross_tiles(zc, 0)[:1]))
        pl.when(zc <= far_z)(lambda: backward_some(zc, cross_tiles(zc, 1)))

    pair_k = (lambda ref: ref.at[:, 0 : chunk // 2], lambda ref: ref.at[:, chunk // 2 : chunk])

    def send_home(parts, into):
        got = []
        for step in range(1, NX):
            there = mod(x + step, NX)
            got.append((links.send(parts.at[there, 0], into.at[x, 0], seq_dev(there, z)), mod(x - step, NX), 0))
        for step in range(NX):
            there = mod(x + step, NX)
            got.append((links.send(parts.at[there, 1], into.at[x, 1], seq_dev(there, far_z)), mod(x - step, NX), 1))
        return got

    def collect(parts, into, got):
        total = [parts[x, 0].astype(F32), 0.0]
        for index, source, a in got:
            links.arrived(index, into.at[source, a])
            total[a] = total[a] + into[source, a].astype(F32)
        return total

    def keep_in(ref):
        def write(value):
            ref[...] = value.astype(ref.dtype)

        return write

    def sums_zx(proj, snd, from_l, from_r, mid, mid_snd, mid_in, write):
        yield from scatter_ring(links, lambda i: proj.at[:, i], lambda i: snd.at[i], lambda i: from_l.at[i],
                                lambda i: from_r.at[i], z, NZ, right_z, left_z,
                                (lambda ref: ref.at[0 : NX // 2], lambda ref: ref.at[NX // 2 : NX]),
                                keep_in(mid))
        mid_snd[...] = mid[...].astype(BF16)
        got = [
            links.send(mid_snd.at[mod(x + step, NX)], mid_in.at[x], seq_dev(mod(x + step, NX), z))
            for step in range(1, NX)
        ]
        yield
        total = mid[x]
        for step in range(1, NX):
            links.arrived(got[step - 1], mid_in.at[mod(x - step, NX)])
            total = total + mid_in[mod(x - step, NX)].astype(F32)
        write(total)

    def sums_xz(proj, snd, from_l, from_r, mid, mid_in, write):
        yield from scatter_ring(links, lambda i: proj.at[i], lambda i: snd.at[i], lambda i: from_l.at[i],
                                lambda i: from_r.at[i], x, NX, right_x, left_x,
                                (lambda ref: ref.at[0 : NZ // 2], lambda ref: ref.at[NZ // 2 : NZ]),
                                keep_in(mid))
        got = [
            links.send(mid.at[mod(z + step, NZ)], mid_in.at[z], seq_dev(x, mod(z + step, NZ)))
            for step in range(1, NZ)
        ]
        yield
        total = mid[z].astype(F32)
        for step in range(1, NZ):
            links.arrived(got[step - 1], mid_in.at[mod(z - step, NZ)])
            total = total + mid_in[mod(z - step, NZ)].astype(F32)
        write(total)

    def spread(part):
        rows = g_t.shape[1] // 2
        cut = (lambda ref: ref.at[0:rows], lambda ref: ref.at[rows : 2 * rows])

        def slot(i, c):
            return g_all.at[i * 2 + c, part]

        own = g_t.at[part]
        ring = gather_ring(links, lambda i: slot(i, core), own, y, 4, right_y, left_y, cut)
        next(ring)
        got = [(links.send(own, slot(y, core), twin), y)]
        g_all[head, part] = g_t[part]
        yield
        next(ring)
        for i in (mod(y - 1, 4), mod(y + 1, 4)):
            got.append((links.send(slot(i, core), slot(i, core), twin), i))
        yield
        for _ in ring:
            pass
        i = mod(y + 2, 4)
        got.append((links.send(slot(i, core), slot(i, core), twin), i))
        yield
        for index, i in got:
            links.arrived(index, slot(i, 1 - core))

    def project(proj, rows):
        def one(i, _):
            part = pl.ds(pl.multiple_of(i * 512, 512), 512)
            proj[i] = nt(x_t[part, :], rows[...]).astype(BF16).reshape(proj.shape[1:])
            return 0

        lax.fori_loop(0, NX, one, 0)

    def write_kv(value):
        gk_out[...] = value[:, 0:64]
        gv_out[...] = value[:, 64:128]

    kv_home = []

    def finish_kv(value):
        kv_home.append(value[0])
        dkv_back[...] = value[1].astype(BF16)
        kv_home.append(links.send(dkv_back, dkv_land, mirror_x))

    kv_ring = scatter_ring(links, lambda i: dkv.at[i], lambda i: dkv_snd.at[i], lambda i: dkv_l.at[i],
                           lambda i: dkv_r.at[i], z, NZ, right_z, left_z, pair_k, finish_kv)
    o_proj = sums_zx(proj_o, po_snd, po_l, po_r, po_x, po_xs, po_xi, keep_in(go_out))
    got_o = send_home(ring_o, o_in)
    slots(backward_slot, (4,))
    pump(kv_ring)
    slots(backward_slot, (3, -3))
    pump(kv_ring)
    for a, rows in enumerate(collect(ring_o, o_in, got_o)):
        for h in range(2):
            o_t[h * 64 : (h + 1) * 64, a * chunk : (a + 1) * chunk] = rows[
                :, h * chunk : (h + 1) * chunk
            ].astype(BF16)

    def project_o(i, _):
        part = pl.ds(pl.multiple_of(i * 512, 512), 512)
        proj_o[i] = nn(o_t[...], g_v[:, part]).T.astype(BF16).reshape(proj_o.shape[1:])
        return 0

    lax.fori_loop(0, NX, project_o, 0)
    pump(o_proj)
    slots(backward_slot, (2, -2))
    pump(kv_ring, o_proj)
    slots(backward_slot, (1, -1))
    pump(kv_ring, o_proj)
    slots(backward_slot, (0,))
    for block in range(NX):
        for a in range(2):
            ring_q[block, a] = (dq_sum[block, a] * 0.125).astype(BF16)
    got_q = send_home(ring_q, q_in)
    pump(kv_ring, o_proj)

    def place_kv(a, rows):
        columns = slice(a * chunk, (a + 1) * chunk)
        g_t[1, 0:64, columns] = turn(rows[0:64], a, -1.0).astype(BF16)
        g_t[1, 64:128, columns] = rows[64:128].astype(BF16)

    place_kv(0, kv_home[0].T)
    pump(o_proj)
    links.arrived(kv_home[1], dkv_land)
    place_kv(1, dkv_land[...].astype(F32).T)
    gather_kv = spread(1)
    pump(gather_kv)
    project(proj_kv, g_t.at[1])
    kv_proj = sums_zx(proj_kv, pk_snd, pk_l, pk_r, pk_x, pk_xs, pk_xi, write_kv)
    pump(kv_proj, o_proj)
    for a, rows in enumerate(collect(ring_q, q_in, got_q)):
        for h in range(2):
            g_t[0, h * 64 : (h + 1) * 64, a * chunk : (a + 1) * chunk] = turn(
                rows[:, h * chunk : (h + 1) * chunk], a, -1.0
            ).astype(BF16)
    gather_q = spread(0)
    pump(gather_q, gather_kv, kv_proj)
    project(proj_q, g_t.at[0])
    q_proj = sums_xz(proj_q, pq_snd, pq_l, pq_r, pq_z, pq_zi, keep_in(gq_out))
    pump(q_proj, kv_proj, gather_kv, q_proj, gather_q, kv_proj, gather_kv, q_proj, kv_proj)

    for index, step in weights:
        links.arrived(index, w_all.at[mod(head - step, NH)])
    gi_sum[...] = sum(nn(w_all[n, :, 128:256], g_all[n, 1]) for n in range(NH))
    together(gather_q, kv_proj, q_proj, o_proj, gather_kv)
    total = gi_sum[...] + sum(nn(w_all[n, :, 0:128], g_all[n, 0]) for n in range(NH))
    gi_out[...] = total.T.astype(BF16)
    links.drain()


def layer(inputs, out_grad, w_query, w_key, w_value, w_output, cos_t, sin_t):
    tokens, model = inputs.shape
    chunk, lanes = tokens // 2, tokens
    slab = model // (NX * NZ)
    tiles = (2 * NX * 2 * NZ) // 2 + 1
    vmem = pl.BlockSpec(memory_space=pltpu.VMEM)
    anywhere = pl.BlockSpec(memory_space=pl.ANY)
    copies = 120

    def vm(*shape, dtype=BF16):
        return pltpu.VMEM(shape, dtype)

    rows = (NX, 2, 64, lanes)

    def sums_zx():
        return [
            vm(NX, NZ, slab, 128), vm(NZ, NX, slab, 128), vm(NZ // 2, NX, slab, 128), vm(NZ // 2, NX, slab, 128),
            vm(NX, slab, 128, dtype=F32), vm(NX, slab, 128), vm(NX, slab, 128),
        ]

    return pl.pallas_call(
        layer_kernel,
        out_shape=(
            jax.ShapeDtypeStruct((tokens, 256), BF16),
            jax.ShapeDtypeStruct((slab, 128), F32),
            jax.ShapeDtypeStruct((slab, 64), F32),
            jax.ShapeDtypeStruct((slab, 64), F32),
            jax.ShapeDtypeStruct((slab, 128), F32),
        ),
        in_specs=[anywhere] * 6 + [vmem] * 2,
        out_specs=(vmem,) * 5,
        scratch_shapes=[
            vm(tokens, model), vm(tokens, model), vm(model, 256), vm(64, model), vm(64, model), vm(128, model),
            vm(NH, model // NH, 256), vm(model, tokens),
            vm(2, 64, lanes), vm(2, 64, lanes), vm(2, chunk, 128),
            vm(*rows), vm(*rows), vm(NZ, 2, chunk, 128), vm(NZ, 2, 128, chunk), vm(NX, 128, 4 * lanes),
            vm(tiles, chunk, lanes), vm(tiles + 7, lanes, dtype=F32), vm(NX, 3, 8, lanes, dtype=F32),
            vm(8, lanes, dtype=F32), vm(8, lanes, dtype=F32), vm(*rows, dtype=F32), vm(*rows, dtype=F32),
            vm(NZ, 2, chunk, 128, dtype=F32),
            vm(*rows), vm(*rows), vm(*rows), vm(*rows), vm(128, tokens), vm(2, 128, tokens),
            vm(NZ, 2, chunk, 128), vm(NZ // 2, 2, chunk, 128), vm(NZ // 2, 2, chunk, 128),
            vm(chunk, 128), vm(chunk, 128),
        ] + sums_zx() + sums_zx() + [
            vm(NX, NZ, slab, 128), vm(NX, NZ, slab, 128), vm(NX // 2, NZ, slab, 128), vm(NX // 2, NZ, slab, 128),
            vm(NZ, slab, 128), vm(NZ, slab, 128),
            vm(NH, 2, 128, tokens), vm(256, tokens, dtype=F32),
            pltpu.SemaphoreType.DMA((copies,)),
            pltpu.SemaphoreType.DMA((copies,)),
            pltpu.SemaphoreType.DMA((6,)),
        ],
        compiler_params=pltpu.CompilerParams(
            collective_id=0, has_side_effects=True, vmem_limit_bytes=60 * 1024 * 1024
        ),
        name="layer",
    )(inputs, out_grad, w_query, w_key, w_value, w_output, cos_t, sin_t)


def hand_on_kernel(*refs):
    count = len(refs) // 2
    for source, target in zip(refs[:count], refs[count:]):
        target[...] = source[...]


def hand_on(arrays):
    vmem = pl.BlockSpec(memory_space=pltpu.VMEM)
    return pl.pallas_call(
        hand_on_kernel,
        out_shape=tuple(jax.ShapeDtypeStruct(array.shape, array.dtype) for array in arrays),
        in_specs=[vmem] * len(arrays),
        out_specs=(vmem,) * len(arrays),
        name="hand_on",
    )(*arrays)


def body(inputs, out_grad, w_query, w_key, w_value, w_output):
    tokens = inputs.shape[0]
    me = lax.axis_index("seq")
    positions = (me * tokens + jnp.arange(tokens, dtype=jnp.int32)).astype(F32)
    cos, sin = rotary(positions)
    results = layer(inputs, out_grad, w_query, w_key.T, w_value.T, w_output, cos.T, sin.T)
    *grads, grad_output = hand_on(results)
    return (*grads, grad_output.T)


def solution(mesh):
    placed = (
        P("seq", None),
        P("seq", None),
        P(None, "head"),
        P(None, "head"),
        P(None, "head"),
        P("head", None),
    )
    return jax.shard_map(
        body,
        mesh=mesh,
        in_specs=placed,
        out_specs=(
            P("seq", "head"),
            P("seq", "head"),
            P("seq", "head"),
            P("seq", "head"),
            P("head", "seq"),
        ),
        check_vma=False,
    )
```

profile of v0, /device:TPU:2, one launch (start us, length us, event | category | flops | bytes accessed | tf_op | source)
XLA Modules:
  0.0 116.0 jit_solution(2301061068700774661)
XLA Ops:
  0.7 1.0 multiply_sine_fusion
  1.6 112.7 %layer.1 = (bf16[512,256]{1,0:T(8,128)(2,1)}, f32[64,128]{1,0:T(8,128)}, f32[64,64]{1,0:T(8,128)}, f32[64,64]{1,0:T(8,128)}, f32[64,128]{1,0:T(8,128)}) custom-call(bf16[512,2048]{1,0:T(8,128)(2,1)} %inputs.1, bf16[512,2048]{1,0:T(8,128)(2,1)} %out_grad.1, bf16[2048,128]{1,0:T(8,128)(2,1)} %w_query.1, bf16[64,2048]{1,0:T(8,128)(2,1)} %bitcast.3, ...), custom_call_target="tpu_custom_call" | custom-call | tf_op jit(solution)/shard_map/layer/pallas_call | solution.py:590
  114.3 1.7 %hand_on.1 = (bf16[512,256]{1,0:T(8,128)(2,1)}, f32[64,128]{1,0:T(8,128)}, f32[64,64]{1,0:T(8,128)}, f32[64,64]{1,0:T(8,128)}, f32[64,128]{1,0:T(8,128)}) custom-call(bf16[512,256]{1,0:T(8,128)(2,1)} %get-tuple-element.15.refs_0_, f32[64,128]{1,0:T(8,128)} %get-tuple-element.16.refs_1_, f32[64,64]{1,0:T(8,128)} %get-tuple-element.17.refs_2_, ...), custom_call_target="tpu_custom_call" | custom-call | tf_op jit(solution)/shard_map/hand_on/pallas_call | solution.py:635
  (2 shorter events, 0.0 us)
where the time goes:
time: 116 us
  Pallas kernels  114 us (98%)
    pallas_call x1, Pallas kernels, layer(): pl.pallas_call(layer_kernel, out_shape=(jax.ShapeDtypeStruct((tokens, 256...  113 us

commit v1 on v0

--- a/solution.py
+++ b/solution.py
@@ -156,11 +156,11 @@
     x_v, g_v, w_cat, wk_v, wv_v, wo_v, w_all, x_t,
     q_own, do_own, kv_own,
     qg, dg, kv, kvt, both, probs, tops, stats, lse, delta, o_sum, dq_sum, dkv,
-    ring_o, o_in, ring_q, q_in, o_t, g_t,
+    ring_o, o_in, o_back, o_land, ring_q, q_in, q_back, q_land, o_t, g_t,
     dkv_snd, dkv_l, dkv_r, dkv_back, dkv_land,
-    proj_o, po_snd, po_l, po_r, po_x, po_xs, po_xi,
-    proj_kv, pk_snd, pk_l, pk_r, pk_x, pk_xs, pk_xi,
-    proj_q, pq_snd, pq_l, pq_r, pq_z, pq_zi,
+    proj_o, po_in, po_mid, po_mid_in,
+    proj_kv, pk_in, pk_mid, pk_mid_in,
+    proj_q, pq_in, pq_mid, pq_mid_in,
     g_all, gi_sum,
     send_sems, recv_sems, copy_sems,
 ):
@@ -195,7 +195,6 @@
     partners = (
         [seq_dev(mod(x + step, NX), z) for step in range(1, NX)]
         + [seq_dev(x, mod(z + step, NZ)) for step in range(1, NZ)]
-        + [seq_dev(mod(x + step, NX), far_z) for step in range(1, NX)]
         + others
     )
     barrier = pltpu.get_barrier_semaphore()
@@ -238,8 +237,14 @@
         for ring in rings:
             next(ring, None)
 
-    q_a, k_a = ring_x(qg, 0, q_own.at[0]), ring_z(0, kv_own.at[0])
-    q_b, k_b = ring_x(qg, 1, qg.at[x, 1]), ring_z(1, kv.at[z, 1])
+    def direct_x(ref, a):
+        got = [links.send(ref.at[x, a], ref.at[x, a], seq_dev(mod(x + step, NX), z)) for step in (2, 1, 3)]
+        yield
+        for n, step in enumerate((2, 1, 3)):
+            links.arrived(got[n], ref.at[mod(x - step, NX), a])
+
+    q_a, k_a = direct_x(qg, 0), ring_z(0, kv_own.at[0])
+    q_b, k_b = direct_x(qg, 1), ring_z(1, kv.at[z, 1])
     d_a, d_b = ring_x(dg, 0, do_own.at[0]), ring_x(dg, 1, dg.at[x, 1])
     pump(q_a, k_a)
     for load in loads[4:]:
@@ -252,24 +257,20 @@
     pump(q_b)
     links.arrived(sent_kv, kv.at[z, 1])
     pump(k_b)
-    sent_do = links.send(do_own.at[1], dg.at[x, 1], mirror_z)
     dkv[...] = jnp.zeros(dkv.shape, F32)
     o_sum[...] = jnp.zeros(o_sum.shape, F32)
     dq_sum[...] = jnp.zeros(dq_sum.shape, F32)
     both[...] = jnp.zeros(both.shape, BF16)
     stats[x, 0] = jnp.full(stats.shape[2:], NEG, F32)
     stats[x, 1] = jnp.zeros(stats.shape[2:], F32)
-    pump(q_a, k_a, q_b, k_b, d_a)
-    links.arrived(sent_do, dg.at[x, 1])
-    pump(d_b)
-
     def flip(n, _):
         part = pl.ds(pl.multiple_of(n * 128, 128), 128)
         x_t[part, :] = x_v[:, part].astype(F32).T.astype(BF16)
         return 0
 
     lax.fori_loop(0, x_t.shape[0] // 128, flip, 0)
-    pump(q_a, q_b)
+    pump(q_a)
+
 
     def full_tiles(zc):
         tiles = []
@@ -310,13 +311,22 @@
             stats[x, 1, group, :] = stats[x, 1, group, :] * keep + total * add
             o_sum[block, a] = o_sum[block, a] * keep + out * add
 
-    def forward_slot(zc):
+    def flip_slot(zc):
         for half in range(2):
             kvt[zc, half] = kv[zc, half].astype(F32).T.astype(BF16)
+
+    def forward_cross(zc, a):
+        if a == 0:
+            pl.when(zc < z)(lambda: forward(zc, cross_tiles(zc, 0)))
+            pl.when(zc == z)(lambda: forward(zc, cross_tiles(zc, 0)[:1], (0,)))
+        else:
+            pl.when(zc <= far_z)(lambda: forward(zc, cross_tiles(zc, 1), (1,)))
+
+    def forward_slot(zc):
+        flip_slot(zc)
         forward(zc, full_tiles(zc))
-        pl.when(zc < z)(lambda: forward(zc, cross_tiles(zc, 0)))
-        pl.when(zc == z)(lambda: forward(zc, cross_tiles(zc, 0)[:1], (0,)))
-        pl.when(zc <= far_z)(lambda: forward(zc, cross_tiles(zc, 1), (1,)))
+        forward_cross(zc, 0)
+        forward_cross(zc, 1)
 
     def slots(work, distances):
         def one(n, _):
@@ -325,14 +335,31 @@
 
         lax.fori_loop(0, len(distances), one, 0)
 
-    slots(forward_slot, (0,))
+    def forward_first(zc):
+        flip_slot(zc)
+        forward(zc, full_tiles(zc)[0::2])
+        forward_cross(zc, 0)
+
+    def forward_second(zc):
+        forward(zc, full_tiles(zc)[1::2])
+        forward_cross(zc, 1)
+
+    slots(forward_first, (0,))
+    pump(k_a, k_b)
+    slots(forward_first, (1, -1))
+    pump(q_b, d_a)
+    sent_do = links.send(do_own.at[1], dg.at[x, 1], mirror_z)
+    slots(forward_second, (0,))
+    slots(forward_second, (1, -1))
+    pump(k_a, k_b)
+    slots(forward_slot, (2, -2))
+    pump(k_a, k_b, d_a)
+    links.arrived(sent_do, dg.at[x, 1])
+    pump(d_b)
+    slots(forward_slot, (3, -3))
     pump(k_a, k_b, d_a, d_b)
-    slots(forward_slot, (1, -1))
-    pump(k_a, k_b, d_a, d_b)
-    slots(forward_slot, (2, -2))
-    pump(k_a, k_b)
-    slots(forward_slot, (3, -3))
     slots(forward_slot, (4,))
+    pump(d_b)
 
     weights = []
     for step in range(1, NH):
@@ -389,34 +416,49 @@
         done = [backward_tile(zc, *tile) for tile in tiles]
         for (half, block, a, _), (p, ds) in zip(tiles, done):
             dq_sum[block, a] += nn(kvt[zc, half, 0:64, :], ds)
-            dkv[zc, half] += nt(ds, both[block, :, a * lanes : (a + 1) * lanes]) + nt(
-                p, both[block, :, (2 + a) * lanes : (3 + a) * lanes]
-            )
+            sides = [both[block, :, n * lanes : (n + 1) * lanes] for n in (a, 2 + a)]
+            dkv[zc, half] += nt(jnp.concatenate([ds, p], 1), jnp.concatenate(sides, 1))
+
+    def backward_cross(zc, a):
+        if a == 0:
+            pl.when(zc < z)(lambda: backward_some(zc, cross_tiles(zc, 0)))
+            pl.when(zc == z)(lambda: backward_some(zc, cross_tiles(zc, 0)[:1]))
+        else:
+            pl.when(zc <= far_z)(lambda: backward_some(zc, cross_tiles(zc, 1)))
+
+    def backward_half(a):
+        def work(zc):
+            backward_some(zc, full_tiles(zc)[a::2])
+            backward_cross(zc, a)
+
+        return work
 
     def backward_slot(zc):
         backward_full(zc)
-        pl.when(zc < z)(lambda: backward_some(zc, cross_tiles(zc, 0)))
-        pl.when(zc == z)(lambda: backward_some(zc, cross_tiles(zc, 0)[:1]))
-        pl.when(zc <= far_z)(lambda: backward_some(zc, cross_tiles(zc, 1)))
+        backward_cross(zc, 0)
+        backward_cross(zc, 1)
 
     pair_k = (lambda ref: ref.at[:, 0 : chunk // 2], lambda ref: ref.at[:, chunk // 2 : chunk])
 
-    def send_home(parts, into):
-        got = []
-        for step in range(1, NX):
-            there = mod(x + step, NX)
-            got.append((links.send(parts.at[there, 0], into.at[x, 0], seq_dev(there, z)), mod(x - step, NX), 0))
-        for step in range(NX):
-            there = mod(x + step, NX)
-            got.append((links.send(parts.at[there, 1], into.at[x, 1], seq_dev(there, far_z)), mod(x - step, NX), 1))
-        return got
-
-    def collect(parts, into, got):
-        total = [parts[x, 0].astype(F32), 0.0]
-        for index, source, a in got:
-            links.arrived(index, into.at[source, a])
-            total[a] = total[a] + into[source, a].astype(F32)
-        return total
+    def home_sums(parts, into, a, back, land, place):
+        order = (2, 1, 3)
+        got = [
+            links.send(parts.at[mod(x + step, NX), a], into.at[x, a], seq_dev(mod(x + step, NX), z))
+            for step in order
+        ]
+        yield
+        total = parts[x, a].astype(F32)
+        for n, step in enumerate(order):
+            source = mod(x - step, NX)
+            links.arrived(got[n], into.at[source, a])
+            total = total + into[source, a].astype(F32)
+        if a == 1:
+            back[...] = total.astype(BF16)
+            sent = links.send(back, land, mirror_z)
+            yield
+            links.arrived(sent, land)
+            total = land[...].astype(F32)
+        place(a, total)
 
     def keep_in(ref):
         def write(value):
@@ -424,37 +466,54 @@
 
         return write
 
-    def sums_zx(proj, snd, from_l, from_r, mid, mid_snd, mid_in, write):
-        yield from scatter_ring(links, lambda i: proj.at[:, i], lambda i: snd.at[i], lambda i: from_l.at[i],
-                                lambda i: from_r.at[i], z, NZ, right_z, left_z,
-                                (lambda ref: ref.at[0 : NX // 2], lambda ref: ref.at[NX // 2 : NX]),
-                                keep_in(mid))
-        mid_snd[...] = mid[...].astype(BF16)
+    def token_sums(proj, into, mid, mid_in, write):
         got = [
-            links.send(mid_snd.at[mod(x + step, NX)], mid_in.at[x], seq_dev(mod(x + step, NX), z))
-            for step in range(1, NX)
+            links.send(proj.at[mod(x + step, NX)], into.at[x], seq_dev(mod(x + step, NX), z))
+            for step in (2, 1, 3)
         ]
         yield
-        total = mid[x]
-        for step in range(1, NX):
-            links.arrived(got[step - 1], mid_in.at[mod(x - step, NX)])
-            total = total + mid_in[mod(x - step, NX)].astype(F32)
-        write(total)
-
-    def sums_xz(proj, snd, from_l, from_r, mid, mid_in, write):
-        yield from scatter_ring(links, lambda i: proj.at[i], lambda i: snd.at[i], lambda i: from_l.at[i],
-                                lambda i: from_r.at[i], x, NX, right_x, left_x,
-                                (lambda ref: ref.at[0 : NZ // 2], lambda ref: ref.at[NZ // 2 : NZ]),
-                                keep_in(mid))
+        total = proj[x].astype(F32)
+        for n, step in enumerate((2, 1, 3)):
+            source = mod(x - step, NX)
+            links.arrived(got[n], into.at[source])
+            total = total + into[source].astype(F32)
+        mid[...] = total.astype(BF16)
+        order = (4, 3, 5, 2, 6, 1, 7)
         got = [
             links.send(mid.at[mod(z + step, NZ)], mid_in.at[z], seq_dev(x, mod(z + step, NZ)))
-            for step in range(1, NZ)
+            for step in order
         ]
         yield
         total = mid[z].astype(F32)
-        for step in range(1, NZ):
-            links.arrived(got[step - 1], mid_in.at[mod(z - step, NZ)])
-            total = total + mid_in[mod(z - step, NZ)].astype(F32)
+        for n, step in enumerate(order):
+            source = mod(z - step, NZ)
+            links.arrived(got[n], mid_in.at[source])
+            total = total + mid_in[source].astype(F32)
+        write(total)
+
+    def token_sums_zx(proj, into, mid, mid_in, write):
+        order = (4, 3, 5, 2, 6, 1, 7)
+        got = [
+            links.send(proj.at[:, mod(z + step, NZ)], into.at[z], seq_dev(x, mod(z + step, NZ)))
+            for step in order
+        ]
+        yield
+        total = proj[:, z].astype(F32)
+        for n, step in enumerate(order):
+            source = mod(z - step, NZ)
+            links.arrived(got[n], into.at[source])
+            total = total + into[source].astype(F32)
+        mid[...] = total.astype(BF16)
+        got = [
+            links.send(mid.at[mod(x + step, NX)], mid_in.at[x], seq_dev(mod(x + step, NX), z))
+            for step in (2, 1, 3)
+        ]
+        yield
+        total = mid[x].astype(F32)
+        for n, step in enumerate((2, 1, 3)):
+            source = mod(x - step, NX)
+            links.arrived(got[n], mid_in.at[source])
+            total = total + mid_in[source].astype(F32)
         write(total)
 
     def spread(part):
@@ -503,67 +562,73 @@
 
     kv_ring = scatter_ring(links, lambda i: dkv.at[i], lambda i: dkv_snd.at[i], lambda i: dkv_l.at[i],
                            lambda i: dkv_r.at[i], z, NZ, right_z, left_z, pair_k, finish_kv)
-    o_proj = sums_zx(proj_o, po_snd, po_l, po_r, po_x, po_xs, po_xi, keep_in(go_out))
-    got_o = send_home(ring_o, o_in)
-    slots(backward_slot, (4,))
-    pump(kv_ring)
-    slots(backward_slot, (3, -3))
-    pump(kv_ring)
-    for a, rows in enumerate(collect(ring_o, o_in, got_o)):
+    def place_o(a, rows):
         for h in range(2):
             o_t[h * 64 : (h + 1) * 64, a * chunk : (a + 1) * chunk] = rows[
                 :, h * chunk : (h + 1) * chunk
             ].astype(BF16)
 
+    def place_q(a, rows):
+        for h in range(2):
+            g_t[0, h * 64 : (h + 1) * 64, a * chunk : (a + 1) * chunk] = turn(
+                rows[:, h * chunk : (h + 1) * chunk], a, -1.0
+            ).astype(BF16)
+
+    def place_kv(a, rows):
+        columns = slice(a * chunk, (a + 1) * chunk)
+        g_t[1, 0:64, columns] = turn(rows[0:64], a, -1.0).astype(BF16)
+        g_t[1, 64:128, columns] = rows[64:128].astype(BF16)
+
     def project_o(i, _):
         part = pl.ds(pl.multiple_of(i * 512, 512), 512)
         proj_o[i] = nn(o_t[...], g_v[:, part]).T.astype(BF16).reshape(proj_o.shape[1:])
         return 0
 
+    o_home, o_home_far = (home_sums(ring_o, o_in, a, o_back, o_land, place_o) for a in range(2))
+    q_home, q_home_far = (home_sums(ring_q, q_in, a, q_back, q_land, place_q) for a in range(2))
+    o_proj = token_sums(proj_o, po_in, po_mid, po_mid_in, keep_in(go_out))
+    kv_proj = token_sums_zx(proj_kv, pk_in, pk_mid, pk_mid_in, write_kv)
+    q_proj = token_sums(proj_q, pq_in, pq_mid, pq_mid_in, keep_in(gq_out))
+    gather_q, gather_kv = spread(0), spread(1)
+
+    def pack_q(a):
+        for block in range(NX):
+            ring_q[block, a] = (dq_sum[block, a] * 0.125).astype(BF16)
+
+    pump(o_home_far, o_home)
+    slots(backward_slot, (4,))
+    pump(kv_ring)
+    slots(backward_slot, (3, -3))
+    pump(kv_ring, o_home_far, o_home)
+    slots(backward_slot, (2, -2))
+    pump(kv_ring, o_home_far)
     lax.fori_loop(0, NX, project_o, 0)
     pump(o_proj)
-    slots(backward_slot, (2, -2))
+    slots(backward_half(1), (1, -1))
+    slots(backward_half(1), (0,))
+    pack_q(1)
+    pump(q_home_far)
+    slots(backward_half(0), (1, -1))
     pump(kv_ring, o_proj)
-    slots(backward_slot, (1, -1))
-    pump(kv_ring, o_proj)
-    slots(backward_slot, (0,))
-    for block in range(NX):
-        for a in range(2):
-            ring_q[block, a] = (dq_sum[block, a] * 0.125).astype(BF16)
-    got_q = send_home(ring_q, q_in)
-    pump(kv_ring, o_proj)
-
-    def place_kv(a, rows):
-        columns = slice(a * chunk, (a + 1) * chunk)
-        g_t[1, 0:64, columns] = turn(rows[0:64], a, -1.0).astype(BF16)
-        g_t[1, 64:128, columns] = rows[64:128].astype(BF16)
-
+    slots(backward_half(0), (0,))
+    pack_q(0)
+    pump(q_home, q_home_far, kv_ring)
     place_kv(0, kv_home[0].T)
-    pump(o_proj)
     links.arrived(kv_home[1], dkv_land)
     place_kv(1, dkv_land[...].astype(F32).T)
-    gather_kv = spread(1)
     pump(gather_kv)
     project(proj_kv, g_t.at[1])
-    kv_proj = sums_zx(proj_kv, pk_snd, pk_l, pk_r, pk_x, pk_xs, pk_xi, write_kv)
-    pump(kv_proj, o_proj)
-    for a, rows in enumerate(collect(ring_q, q_in, got_q)):
-        for h in range(2):
-            g_t[0, h * 64 : (h + 1) * 64, a * chunk : (a + 1) * chunk] = turn(
-                rows[:, h * chunk : (h + 1) * chunk], a, -1.0
-            ).astype(BF16)
-    gather_q = spread(0)
-    pump(gather_q, gather_kv, kv_proj)
+    pump(kv_proj, q_home, q_home_far, gather_q)
     project(proj_q, g_t.at[0])
-    q_proj = sums_xz(proj_q, pq_snd, pq_l, pq_r, pq_z, pq_zi, keep_in(gq_out))
-    pump(q_proj, kv_proj, gather_kv, q_proj, gather_q, kv_proj, gather_kv, q_proj, kv_proj)
-
+    pump(q_proj, gather_kv, gather_q, gather_kv, gather_q, gather_kv)
     for index, step in weights:
         links.arrived(index, w_all.at[mod(head - step, NH)])
     gi_sum[...] = sum(nn(w_all[n, :, 128:256], g_all[n, 1]) for n in range(NH))
-    together(gather_q, kv_proj, q_proj, o_proj, gather_kv)
+    pump(gather_q, q_proj)
     total = gi_sum[...] + sum(nn(w_all[n, :, 0:128], g_all[n, 0]) for n in range(NH))
     gi_out[...] = total.T.astype(BF16)
+    pump(kv_proj)
+    together(q_proj, kv_proj, o_proj)
     links.drain()
 
 
@@ -581,12 +646,7 @@
 
     rows = (NX, 2, 64, lanes)
 
-    def sums_zx():
-        return [
-            vm(NX, NZ, slab, 128), vm(NZ, NX, slab, 128), vm(NZ // 2, NX, slab, 128), vm(NZ // 2, NX, slab, 128),
-            vm(NX, slab, 128, dtype=F32), vm(NX, slab, 128), vm(NX, slab, 128),
-        ]
-
+    sums = [vm(NX, NZ, slab, 128), vm(NX, NZ, slab, 128), vm(NZ, slab, 128), vm(NZ, slab, 128)]
     return pl.pallas_call(
         layer_kernel,
         out_shape=(
@@ -606,12 +666,13 @@
             vm(tiles, chunk, lanes), vm(tiles + 7, lanes, dtype=F32), vm(NX, 3, 8, lanes, dtype=F32),
             vm(8, lanes, dtype=F32), vm(8, lanes, dtype=F32), vm(*rows, dtype=F32), vm(*rows, dtype=F32),
             vm(NZ, 2, chunk, 128, dtype=F32),
-            vm(*rows), vm(*rows), vm(*rows), vm(*rows), vm(128, tokens), vm(2, 128, tokens),
+            vm(*rows), vm(*rows), vm(64, lanes), vm(64, lanes), vm(*rows), vm(*rows), vm(64, lanes), vm(64, lanes),
+            vm(128, tokens), vm(2, 128, tokens),
             vm(NZ, 2, chunk, 128), vm(NZ // 2, 2, chunk, 128), vm(NZ // 2, 2, chunk, 128),
             vm(chunk, 128), vm(chunk, 128),
-        ] + sums_zx() + sums_zx() + [
-            vm(NX, NZ, slab, 128), vm(NX, NZ, slab, 128), vm(NX // 2, NZ, slab, 128), vm(NX // 2, NZ, slab, 128),
-            vm(NZ, slab, 128), vm(NZ, slab, 128),
+        ] + sums + [
+            vm(NX, NZ, slab, 128), vm(NZ, NX, slab, 128), vm(NX, slab, 128), vm(NX, slab, 128),
+        ] + sums + [
             vm(NH, 2, 128, tokens), vm(256, tokens, dtype=F32),
             pltpu.SemaphoreType.DMA((copies,)),
             pltpu.SemaphoreType.DMA((copies,)),

time: 116 us -> 104 us (0.90); the launches traced: 116 us -> 102 us
  Pallas kernels: 114 us -> 100 us
    pallas_call x1, Pallas kernels: 113 us -> 98.3 us  [layer(): pl.pallas_call(layer_kernel, out_shape=(jax.ShapeDtypeStruct((tokens, 256...]
where the time goes in v1:
time: 104 us; the launch traced here: 102 us
  Pallas kernels  100 us (96%)
    pallas_call x1, Pallas kernels, layer(): pl.pallas_call(layer_kernel, out_shape=(jax.ShapeDtypeStruct((tokens, 256...  98.3 us

profile of v1, /device:TPU:2, one launch (start us, length us, event | category | flops | bytes accessed | tf_op | source)
XLA Modules:
  0.0 101.7 jit_solution(1309280337740071404)
XLA Ops:
  0.7 1.0 multiply_sine_fusion
  1.6 98.3 %layer.1 = (bf16[512,256]{1,0:T(8,128)(2,1)}, f32[64,128]{1,0:T(8,128)}, f32[64,64]{1,0:T(8,128)}, f32[64,64]{1,0:T(8,128)}, f32[64,128]{1,0:T(8,128)}) custom-call(bf16[512,2048]{1,0:T(8,128)(2,1)} %inputs.1, bf16[512,2048]{1,0:T(8,128)(2,1)} %out_grad.1, bf16[2048,128]{1,0:T(8,128)(2,1)} %w_query.1, bf16[64,2048]{1,0:T(8,128)(2,1)} %bitcast.3, ...), custom_call_target="tpu_custom_call" | custom-call | tf_op jit(solution)/shard_map/layer/pallas_call | solution.py:650
  99.9 1.7 %hand_on.1 = (bf16[512,256]{1,0:T(8,128)(2,1)}, f32[64,128]{1,0:T(8,128)}, f32[64,64]{1,0:T(8,128)}, f32[64,64]{1,0:T(8,128)}, f32[64,128]{1,0:T(8,128)}) custom-call(bf16[512,256]{1,0:T(8,128)(2,1)} %get-tuple-element.15.refs_0_, f32[64,128]{1,0:T(8,128)} %get-tuple-element.16.refs_1_, f32[64,64]{1,0:T(8,128)} %get-tuple-element.17.refs_2_, ...), custom_call_target="tpu_custom_call" | custom-call | tf_op jit(solution)/shard_map/hand_on/pallas_call | solution.py:696
  (2 shorter events, 0.0 us)
